TPU v7x, 32 devices: a whole 2x2x4 slice. The times are simulated.
32 devices in a mesh: batch: 8 (over y, x, core), seq: 4 (over z).
Axes of the slice: x: 2, y: 2, z: 4, core: 2. Of those that a mesh axis runs over, the one named last changes fastest.
Arguments:
- tokens: bfloat16 [8, 8192, 512], P('batch', 'seq'), may hold values from -6 to 6
- cotangent: bfloat16 [8, 8192, 512], P('batch', 'seq'), may hold values from -6 to 6
- segment: int32 [8, 8192], P('batch', 'seq'), may hold values from 0 to 65, as said below
- keep_mask: int32 [8, 8192], P('batch', 'seq'), may hold values from 0 to 1, as said below
- attn_master: float32 [512, 1536], P(('batch', 'seq')), may hold values from -0.25 to 0.25
- out_master: float32 [512, 512], P(('batch', 'seq')), may hold values from -2 to 2
- in_master: float32 [512, 2048], P(('batch', 'seq')), may hold values from -0.25 to 0.25
- back_master: float32 [2048, 512], P(('batch', 'seq')), may hold values from -0.125 to 0.125
- vec_master: float32 [12, 512], P(None, ('batch', 'seq')), may hold values from -0.6 to 1.4
- attn_first: float32 [512, 1536], P(('batch', 'seq')), may hold values from -160 to 160
- out_first: float32 [512, 512], P(('batch', 'seq')), may hold values from -32 to 32
- in_first: float32 [512, 2048], P(('batch', 'seq')), may hold values from -40 to 40
- back_first: float32 [2048, 512], P(('batch', 'seq')), may hold values from -96 to 96
- vec_first: float32 [12, 512], P(None, ('batch', 'seq')), may hold values from -160 to 160
- attn_second: float32 [512, 1536], P(('batch', 'seq')), may hold values from 32.768 to 524.288
- out_second: float32 [512, 512], P(('batch', 'seq')), may hold values from 1.31072 to 20.97152
- in_second: float32 [512, 2048], P(('batch', 'seq')), may hold values from 1.96608 to 32.768
- back_second: float32 [2048, 512], P(('batch', 'seq')), may hold values from 11.79648 to 190.0544
- vec_second: float32 [12, 512], P(None, ('batch', 'seq')), may hold values from 32.768 to 524.288
Outputs:
- output: bfloat16 [8, 8192, 512], P('batch', 'seq')
- input_grad: float32 [8, 8192, 512], P('batch', 'seq')
- attn_first_new: float32 [512, 1536], P(('batch', 'seq'))
- out_first_new: float32 [512, 512], P(('batch', 'seq'))
- in_first_new: float32 [512, 2048], P(('batch', 'seq'))
- back_first_new: float32 [2048, 512], P(('batch', 'seq'))
- vec_first_new: float32 [12, 512], P(None, ('batch', 'seq'))
- attn_second_new: float32 [512, 1536], P(('batch', 'seq'))
- out_second_new: float32 [512, 512], P(('batch', 'seq'))
- in_second_new: float32 [512, 2048], P(('batch', 'seq'))
- back_second_new: float32 [2048, 512], P(('batch', 'seq'))
- vec_second_new: float32 [12, 512], P(None, ('batch', 'seq'))
- attn_master_new: float32 [512, 1536], P(('batch', 'seq'))
- out_master_new: float32 [512, 512], P(('batch', 'seq'))
- in_master_new: float32 [512, 2048], P(('batch', 'seq'))
- back_master_new: float32 [2048, 512], P(('batch', 'seq'))
- vec_master_new: float32 [12, 512], P(None, ('batch', 'seq'))
- attn_copy: bfloat16 [512, 1536], P(None, 'seq')
- out_copy: bfloat16 [512, 512], P(None, 'seq')
- in_copy: bfloat16 [512, 2048], P(None, 'seq')
- back_copy: bfloat16 [2048, 512], P(None, 'seq')
- vec_copy: bfloat16 [12, 512], P(None, 'seq')
Inputs may be any that keep to these rules, and one draw needn't show every extreme that they name: Segment numbers of a stream start at 0 and rise by one from a segment to the next; each segment holds 5 to 250 positions, and the first segment of every stream holds exactly 250. Segments come in consecutive pairs (0 and 1, 2 and 3, ...) of 255 positions together; the stream's last position lies in the last segment, which every stream reaches. keep_mask is 1 at the first position of every segment, and within a segment no 1 follows a 0.
All inputs are finite; a program needn't handle non-finite values.
Results may differ from a plain program's by a relative error of at most 0.012.
The roundings to bfloat16 on the way count: a program that leaves them out, or rounds other values in their place, can miss the bound.
Values may be sent and summed in bfloat16 or wider, within the bound.
A program may use at most 320 MiB of HBM per device.

v0:
```python
import functools
import math

import jax
import jax.numpy as jnp
from jax import lax
from jax.experimental import pallas as pl
from jax.experimental.pallas import tpu as pltpu
from jax.sharding import PartitionSpec as P

D = 512
HEADS = 8
HEAD_DIM = 64
FF = 2048
STEP = 10
PAIR = 255
SLOT = 256
HALO = 64
TILES = 4
TAIL = 64
PIECE = TAIL // TILES
TILE = 2 * SLOT + PIECE
ROWS = TILES * TILE
LANES = 8 * SLOT + 128
AUG = 16
MIB = 1 << 20

norm_epsilon = 1e-05
beta_first = 0.9
beta_second = 0.999
adam_epsilon = 1e-08
weight_decay = 0.01
learn_rates = (0.03, 0.2, 0.03, 0.02, 0.5)
big = 1e30

f32 = jnp.float32
bf16 = jnp.bfloat16


def dot(a, b, ca, cb):
    return lax.dot_general(a, b, (((ca,), (cb,)), ((), ())), preferred_element_type=f32)


def adam_update(master, first, second, gradient, rate):
    first_new = beta_first * first + (1.0 - beta_first) * gradient
    second_new = beta_second * second + (1.0 - beta_second) * gradient * gradient
    first_hat = first_new / (1.0 - beta_first**STEP)
    second_hat = second_new / (1.0 - beta_second**STEP)
    master_new = master - rate * (
        first_hat / (jnp.sqrt(second_hat) + adam_epsilon) + weight_decay * master
    )
    return (first_new, second_new, master_new)


def slot_row(j):
    return pl.multiple_of((j // 2) * TILE + (j % 2) * SLOT, 16)


def first_row(j, seq):
    return HALO + PAIR * j - 8 * seq


def staged(ref, start):
    base = pl.multiple_of((start // 16) * 16, 16)
    rest = start - base
    wide = ref[pl.ds(base, SLOT + 16), :].astype(f32)
    wide = jnp.where(rest >= 8, wide[8:], wide[:-8])
    shift = rest % 8
    groups = (SLOT + 8) // 8
    wide = wide.reshape(groups, 8, D)
    turned = pltpu.roll(wide, lax.rem(8 - shift, 8), 1)
    place = lax.broadcasted_iota(jnp.int32, (groups - 1, 8, D), 1)
    block = jnp.where(place < 8 - shift, turned[:-1], turned[1:]).reshape(SLOT, D)
    row = lax.broadcasted_iota(jnp.int32, (SLOT, D), 0)
    return jnp.where(row < PAIR, block, 0.0).astype(bf16)


def unstage(ref, start, block):
    base = pl.multiple_of((start // 8) * 8, 8)
    shift = start - base
    turned = pltpu.roll(block.reshape(SLOT // 8, 8, D), shift, 1)
    place = lax.broadcasted_iota(jnp.int32, (1, 8, D), 1)
    keep = ref[pl.ds(base, 8), :].reshape(1, 8, D)
    low = jnp.concatenate([keep, turned], 0)
    high = jnp.concatenate([turned, turned[-1:]], 0)
    place = lax.broadcasted_iota(jnp.int32, low.shape, 1)
    ref[pl.ds(base, SLOT + 8), :] = jnp.where(place < shift, low, high).reshape(SLOT + 8, D)


def stage_slot(ref, start, out_ref, row):
    base = pl.multiple_of((start // 16) * 16, 16)
    rest = start - base
    shift = rest % 8
    groups = (SLOT + 8) // 8
    place = lax.broadcasted_iota(jnp.int32, (groups - 1, 8, 128), 1)
    number = lax.broadcasted_iota(jnp.int32, (groups - 1, 8, 128), 0) * 8 + place
    for g in range(D // 128):
        cols = slice(g * 128, (g + 1) * 128)
        wide = ref[pl.ds(base, SLOT + 16), cols].astype(f32)
        wide = jnp.where(rest >= 8, wide[8:], wide[:-8]).reshape(groups, 8, 128)
        turned = pltpu.roll(wide, lax.rem(8 - shift, 8), 1)
        block = jnp.where(place < 8 - shift, turned[:-1], turned[1:])
        block = jnp.where(number < PAIR, block, 0.0)
        out_ref[pl.ds(row, SLOT), cols] = block.reshape(SLOT, 128).astype(bf16)


def unstage_slot(ref, start, column):
    base = pl.multiple_of((start // 8) * 8, 8)
    shift = start - base
    for g in range(D // 128):
        cols = slice(g * 128, (g + 1) * 128)
        turned = pltpu.roll(column(g).reshape(SLOT // 8, 8, 128), shift, 1)
        keep = ref[pl.ds(base, 8), cols].reshape(1, 8, 128)
        low = jnp.concatenate([keep, turned], 0)
        high = jnp.concatenate([turned, turned[-1:]], 0)
        place = lax.broadcasted_iota(jnp.int32, low.shape, 1)
        ref[pl.ds(base, SLOT + 8), cols] = jnp.where(place < shift, low, high).reshape(SLOT + 8, 128)


def tail_rows(ref, count, is_last):
    kept = ref[HALO + 2048 - count : HALO + 2048, :].astype(f32)
    if count < TAIL:
        kept = jnp.concatenate([kept, jnp.zeros((TAIL - count, D), f32)], 0)
    return jnp.where(is_last, kept, 0.0).astype(bf16)


def tag_rows(tag, pair):
    width = tag.shape[1]
    number = tag // 2 - 2 * pair
    kept = tag % 2
    row = lax.broadcasted_iota(jnp.int32, (AUG, width), 0)
    match = row == number
    query = jnp.where(match, 1.0, 0.0).astype(bf16)
    key = jnp.where(match & (kept == 1), 0.0, -big)
    key = jnp.where(row < 4, key, 0.0).astype(bf16)
    return query, key


def attn_forward_kernel(
    seq_count, tok_ref, cot_ref, tok_halo, cot_halo, seg_ref, keep_ref, seg_halo, keep_halo,
    w_ref, vec_ref,
    xs_ref, es_ref, xt_ref, qt_ref, kt_ref, vt_ref, c_ref, lse_ref,
    wt_ref, x_ref, e_ref, tag_ref, sems,
):
    seq = lax.axis_index("seq")
    is_last = seq == seq_count - 1
    rows = tok_ref.shape[1]
    loads = []
    for i, (whole, halo, ext) in enumerate(((tok_ref, tok_halo, x_ref), (cot_ref, cot_halo, e_ref))):
        loads.append(pltpu.make_async_copy(whole.at[0], ext.at[pl.ds(HALO, rows)], sems.at[2 * i]))
        loads.append(pltpu.make_async_copy(halo, ext.at[pl.ds(0, HALO)], sems.at[2 * i + 1]))
    for load in loads:
        load.start()
    for part in range(3):
        wt_ref[part * D : (part + 1) * D, :] = w_ref[:, part * D : (part + 1) * D].T
    tag_ref[...] = jnp.zeros_like(tag_ref)
    edge = seg_halo[...] * 2 + keep_halo[...]
    tag_ref[:, :HALO] = jnp.broadcast_to(edge[:, 128 - HALO :], (8, HALO))
    tag_ref[:, HALO : HALO + rows] = jnp.broadcast_to(seg_ref[...] * 2 + keep_ref[...], (8, rows))
    query_bias = vec_ref[:, 0:1].astype(f32)
    value_bias = vec_ref[:, 1:2].astype(f32)
    for load in loads:
        load.wait()

    def block(xb, tag, pair, lane, width):
        lanes = pl.ds(lane, width)
        xt_ref[:D, lanes] = xb.T
        q = dot(wt_ref[:D, :], xb, 1, 1) + query_bias
        q = (q.astype(bf16).astype(f32) * HEAD_DIM**-0.5).astype(bf16)
        k = dot(wt_ref[D : 2 * D, :], xb, 1, 1).astype(bf16)
        v = (dot(wt_ref[2 * D :, :], xb, 1, 1) + value_bias).astype(bf16)
        query_tag, key_tag = tag_rows(tag, pair)
        vt_ref[:, lanes] = v
        context = []
        for h in range(HEADS):
            rows = slice(h * HEAD_DIM, (h + 1) * HEAD_DIM)
            qh = jnp.concatenate([q[rows], query_tag], 0)
            kh = jnp.concatenate([k[rows], key_tag], 0)
            qt_ref[h, :, lanes] = qh
            kt_ref[h, :, lanes] = kh
            s = dot(kh, qh, 0, 0)
            top = jnp.max(s, axis=0, keepdims=True)
            ex = jnp.exp(s - top)
            total = jnp.sum(ex, axis=0, keepdims=True)
            lse_ref[h : h + 1, lanes] = top + jnp.log(total)
            a = (ex * (1.0 / total)).astype(bf16)
            context.append(dot(v[rows], a, 1, 0))
        return jnp.concatenate(context, 0).astype(bf16).T

    def one(j, carry):
        start = first_row(j, seq)
        row = slot_row(j)
        xb = staged(x_ref, start)
        xs_ref[pl.ds(row, SLOT), :] = xb
        es_ref[pl.ds(row, SLOT), :] = staged(e_ref, start)
        wide = tag_ref[:, pl.ds(pl.multiple_of(j * SLOT, 128), SLOT + 128)]
        width = SLOT + 128
        tag = pltpu.roll(wide, width - (start - j * SLOT), 1)[:1, :SLOT]
        c_ref[pl.ds(row, SLOT), :] = block(
            xb, tag, 8 * seq + j, pl.multiple_of(j * SLOT, 128), SLOT
        )
        return carry

    lax.fori_loop(0, 8, one, 0)
    count = 8 * seq_count
    xt_ref[:, 8 * SLOT :] = jnp.zeros((D + AUG, 128), bf16)
    xb = tail_rows(x_ref, count, is_last)
    eb = tail_rows(e_ref, count, is_last)
    tag = tag_ref[:1, 2048:2176]
    tag = pltpu.roll(tag_ref[:, 2048:2176], 128 - (64 - count), 1)[:1, :TAIL] if count < 64 else tag[:, :TAIL]
    place = lax.broadcasted_iota(jnp.int32, (1, TAIL), 1)
    tag = jnp.where(place < count, tag, (2 * 8 * seq_count + 3) * 2)
    cb = block(xb, tag, 8 * seq_count, 8 * SLOT, TAIL)
    for t in range(TILES):
        rows = slice(t * PIECE, (t + 1) * PIECE)
        at = slice(t * TILE + 2 * SLOT, (t + 1) * TILE)
        xs_ref[at, :] = xb[rows]
        es_ref[at, :] = eb[rows]
        c_ref[at, :] = cb[rows]
    ones = lax.broadcasted_iota(jnp.int32, (AUG, LANES), 0) == 0
    xt_ref[D:, :] = jnp.where(ones, 1.0, 0.0).astype(bf16)


def attn_forward(seq_count, tokens, cotangent, *others):
    shape = jax.ShapeDtypeStruct
    vmem = pl.BlockSpec(memory_space=pltpu.VMEM)
    hbm = pl.BlockSpec(memory_space=pl.ANY)
    return pl.pallas_call(
        functools.partial(attn_forward_kernel, seq_count),
        out_shape=(
            shape((ROWS, D), bf16),
            shape((ROWS, D), bf16),
            shape((D + AUG, LANES), bf16),
            shape((HEADS, HEAD_DIM + AUG, LANES), bf16),
            shape((HEADS, HEAD_DIM + AUG, LANES), bf16),
            shape((D, LANES), bf16),
            shape((ROWS, D), bf16),
            shape((HEADS, LANES), f32),
        ),
        in_specs=[hbm, hbm] + [vmem] * len(others),
        out_specs=[vmem] * 8,
        scratch_shapes=[
            pltpu.VMEM((3 * D, D), bf16),
            pltpu.VMEM((HALO + tokens.shape[1], D), bf16),
            pltpu.VMEM((HALO + tokens.shape[1], D), bf16),
            pltpu.VMEM((8, LANES), jnp.int32),
            pltpu.SemaphoreType.DMA((4,)),
        ],
        compiler_params=pltpu.CompilerParams(vmem_limit_bytes=56 * MIB),
        name="attn_forward",
    )(tokens, cotangent, *others)


def feed_kernel(
    xs_ref, c_ref, es_ref, wo_ref, w1_ref, w2_ref, vect_ref,
    z_ref, dh_ref, dr_ref, gwo_ref, gw1_ref, gw2_ref, gvec_ref, gb1_ref,
    u_ref, g_ref, awo_ref, aw1_ref, aw2_ref, vec_ref,
):
    step = pl.program_id(0)

    @pl.when(step == 0)
    def _():
        awo_ref[...] = jnp.zeros_like(awo_ref)
        aw1_ref[...] = jnp.zeros_like(aw1_ref)
        aw2_ref[...] = jnp.zeros_like(aw2_ref)
        gvec_ref[...] = jnp.zeros_like(gvec_ref)
        gb1_ref[...] = jnp.zeros_like(gb1_ref)
        vec_ref[...] = vect_ref[...].astype(f32).T

    def mean(v):
        return jnp.mean(v, axis=-1, keepdims=True)

    def row_sum(v):
        return jnp.sum(v, axis=0, keepdims=True)

    bo, b2, g1, c1, g2, c2 = (vec_ref[i : i + 1, :] for i in range(2, 8))
    h1 = xs_ref[...].astype(f32) + (dot(c_ref[...], wo_ref[...], 1, 0) + bo)
    mid = h1 - mean(h1)
    inv1 = lax.rsqrt(mean(mid * mid) + norm_epsilon)
    n1 = mid * inv1
    y = n1 * g1 + c1
    yb = y.astype(bf16)
    chunk = D
    f = None
    for k in range(FF // chunk):
        cols = slice(k * chunk, (k + 1) * chunk)
        u = dot(yb, w1_ref[:, cols], 1, 0) + vec_ref[8 + k : 9 + k, :]
        cdf = 0.5 * (1.0 + lax.erf(u * 0.7071067811865476))
        gk = (u * cdf).astype(bf16)
        u_ref[:, cols] = cdf + u * jnp.exp(u * u * -0.5) * 0.3989422804014327
        g_ref[:, cols] = gk
        part = dot(gk, w2_ref[cols, :], 1, 0)
        f = part if f is None else f + part
    h2 = y + (f + b2)
    mid2 = h2 - mean(h2)
    inv2 = lax.rsqrt(mean(mid2 * mid2) + norm_epsilon)
    n2 = mid2 * inv2
    z_ref[...] = (n2 * g2 + c2).astype(bf16)
    e = es_ref[...].astype(f32)
    gvec_ref[7:8, :] += row_sum(e)
    gvec_ref[6:7, :] += row_sum(e * n2)
    eg = e * g2
    dh2 = (eg - mean(eg) - n2 * mean(eg * n2)) * inv2
    df = dh2.astype(bf16)
    gvec_ref[3:4, :] += row_sum(df.astype(f32))
    dft = df.T
    ybt = yb.T
    dy = dh2
    for k in range(FF // chunk):
        cols = slice(k * chunk, (k + 1) * chunk)
        aw2_ref[:, cols] += dot(dft, g_ref[:, cols], 1, 0)
        dg = dot(df, w2_ref[cols, :], 1, 1)
        du = (dg * u_ref[:, cols]).astype(bf16)
        gb1_ref[:1, cols] += row_sum(du.astype(f32))
        aw1_ref[:, cols] += dot(ybt, du, 1, 0)
        dy = dy + dot(du, w1_ref[:, cols], 1, 1)
    gvec_ref[5:6, :] += row_sum(dy)
    gvec_ref[4:5, :] += row_sum(dy * n1)
    eg = dy * g1
    dh1 = (eg - mean(eg) - n1 * mean(eg * n1)) * inv1
    dh_ref[...] = dh1
    dr = dh1.astype(bf16)
    dr_ref[...] = dr
    gvec_ref[2:3, :] += row_sum(dr.astype(f32))
    awo_ref[...] += dot(c_ref[...].T, dr, 1, 0)

    @pl.when(step == TILES - 1)
    def _():
        gwo_ref[...] = awo_ref[...].astype(bf16)
        gw1_ref[...] = aw1_ref[...].astype(bf16)
        for k in range(FF // chunk):
            cols = slice(k * chunk, (k + 1) * chunk)
            gw2_ref[cols, :] = aw2_ref[:, cols].astype(bf16).T


def feed(xs, c, es, wo, w1, w2, vec_t):
    shape = jax.ShapeDtypeStruct
    tile = pl.BlockSpec((TILE, D), lambda i: (i, 0))

    def whole(*dims):
        return pl.BlockSpec(dims, lambda i: (0,) * len(dims), pipeline_mode=pl.Buffered(1))

    return pl.pallas_call(
        feed_kernel,
        grid=(TILES,),
        out_shape=(
            shape((ROWS, D), bf16),
            shape((ROWS, D), f32),
            shape((ROWS, D), bf16),
            shape((D, D), bf16),
            shape((D, FF), bf16),
            shape((FF, D), bf16),
            shape((8, D), f32),
            shape((8, FF), f32),
        ),
        in_specs=[tile, tile, tile, whole(D, D), whole(D, FF), whole(FF, D), whole(D, 128)],
        out_specs=[tile, tile, tile, whole(D, D), whole(D, FF), whole(FF, D), whole(8, D), whole(8, FF)],
        scratch_shapes=[
            pltpu.VMEM((TILE, FF), f32),
            pltpu.VMEM((TILE, FF), bf16),
            pltpu.VMEM((D, D), f32),
            pltpu.VMEM((D, FF), f32),
            pltpu.VMEM((D, FF), f32),
            pltpu.VMEM((128, D), f32),
        ],
        compiler_params=pltpu.CompilerParams(vmem_limit_bytes=60 * MIB),
        name="feed",
    )(xs, c, es, wo, w1, w2, vec_t)


def attn_backward_kernel(
    seq_count, xt_ref, qt_ref, kt_ref, vt_ref, lse_ref, dr_ref, dh_ref, z_ref, w_ref, wo_ref,
    out_ref, out_halo_ref, in_ref, in_halo_ref, gwa_ref, gbias_ref,
    dpt_ref, ext_ref,
):
    seq = lax.axis_index("seq")
    is_last = seq == seq_count - 1

    def block(dr, lane, width):
        lanes = pl.ds(lane, width)
        dct = dot(wo_ref[...], dr, 1, 1).astype(bf16)
        for h in range(HEADS):
            rows = slice(h * HEAD_DIM, (h + 1) * HEAD_DIM)
            qh = qt_ref[h, :, lanes]
            kh = kt_ref[h, :, lanes]
            vh = vt_ref[rows, lanes]
            dch = dct[rows]
            a = jnp.exp(dot(kh, qh, 0, 0) - lse_ref[h : h + 1, lanes])
            da = dot(vh, dch, 0, 0)
            ada = a * da
            ds = (ada - a * jnp.sum(ada, axis=0, keepdims=True)).astype(bf16)
            dv = dot(dch, a.astype(bf16), 1, 1)
            dk = dot(qh[:HEAD_DIM], ds, 1, 1)
            dq = dot(kh[:HEAD_DIM], ds, 1, 0) * HEAD_DIM**-0.5
            dpt_ref[rows, lanes] = dq.astype(bf16)
            dpt_ref[slice(D + h * HEAD_DIM, D + (h + 1) * HEAD_DIM), lanes] = dk.astype(bf16)
            dpt_ref[slice(2 * D + h * HEAD_DIM, 2 * D + (h + 1) * HEAD_DIM), lanes] = dv.astype(bf16)
        return dot(w_ref[...], dpt_ref[:, lanes], 1, 0).T

    dpt_ref[:, 8 * SLOT :] = jnp.zeros((3 * D, 128), bf16)

    def one(j, carry):
        row = slot_row(j)
        grad = block(dr_ref[pl.ds(row, SLOT), :], pl.multiple_of(j * SLOT, 128), SLOT)
        unstage(ext_ref, first_row(j, seq), grad + dh_ref[pl.ds(row, SLOT), :])
        return carry

    lax.fori_loop(0, 8, one, 0)
    count = 8 * seq_count

    def tail_of(ref):
        return jnp.concatenate(
            [ref[t * TILE + 2 * SLOT : (t + 1) * TILE, :] for t in range(TILES)], 0
        )

    grad = block(tail_of(dr_ref), 8 * SLOT, TAIL) + tail_of(dh_ref)

    @pl.when(is_last)
    def _():
        ext_ref[HALO + 2048 - count : HALO + 2048, :] = grad[:count]

    in_halo_ref[...] = ext_ref[:HALO, :]
    in_ref[...] = ext_ref[HALO : HALO + 2048, :]

    def two(j, carry):
        unstage(ext_ref, first_row(j, seq), z_ref[pl.ds(slot_row(j), SLOT), :].astype(f32))
        return carry

    lax.fori_loop(0, 8, two, 0)
    tail = tail_of(z_ref).astype(f32)

    @pl.when(is_last)
    def _():
        ext_ref[HALO + 2048 - count : HALO + 2048, :] = tail[:count]

    out_halo_ref[...] = ext_ref[:HALO, :].astype(bf16)
    out_ref[...] = ext_ref[HALO : HALO + 2048, :].astype(bf16)
    for part in range(3):
        cols = slice(part * D, (part + 1) * D)
        g = dot(xt_ref[...], dpt_ref[cols, :], 1, 1)
        gwa_ref[:, cols] = g[:D].astype(bf16)
        gbias_ref[:, cols] = g[D : D + 8]


def attn_backward(seq_count, *operands):
    shape = jax.ShapeDtypeStruct
    return pl.pallas_call(
        functools.partial(attn_backward_kernel, seq_count),
        out_shape=(
            shape((2048, D), bf16),
            shape((HALO, D), bf16),
            shape((2048, D), f32),
            shape((HALO, D), f32),
            shape((D, 3 * D), bf16),
            shape((8, 3 * D), f32),
        ),
        in_specs=[pl.BlockSpec(memory_space=pltpu.VMEM)] * len(operands),
        out_specs=[pl.BlockSpec(memory_space=pltpu.VMEM)] * 6,
        scratch_shapes=[
            pltpu.VMEM((3 * D, LANES), bf16),
            pltpu.VMEM((HALO + 2048 + 16, D), f32),
        ],
        compiler_params=pltpu.CompilerParams(vmem_limit_bytes=60 * MIB),
        name="attn_backward",
    )(*operands)


MESH = pl.DeviceIdType.MESH
PLANE = 4
DEPTH = 4


class Place:
    def __init__(self):
        self.batch = lax.axis_index("batch")
        self.z = lax.axis_index("seq")
        self.core = self.batch % 2
        self.plane = self.batch // 2

    def plane_at(self, k):
        x = (self.plane % 2 + k % 2) % 2
        y = (self.plane // 2 + k // 2) % 2
        return y * 2 + x

    def in_plane(self, k, other=0):
        core = self.core if other == 0 else 1 - self.core
        return {"batch": self.plane_at(k) * 2 + core, "seq": self.z}

    def depth_at(self, k):
        return (self.z + k) % DEPTH

    def in_depth(self, k):
        return {"batch": self.batch, "seq": self.depth_at(k)}

    def sibling(self):
        return {"batch": self.plane * 2 + 1 - self.core, "seq": self.z}

    def greet(self):
        barrier = pltpu.get_barrier_semaphore()
        for k in range(1, 4):
            pl.semaphore_signal(barrier, inc=1, device_id=self.in_plane(k), device_id_type=MESH)
            pl.semaphore_signal(barrier, inc=1, device_id=self.in_depth(k), device_id_type=MESH)
            pl.semaphore_signal(barrier, inc=1, device_id=self.in_plane(k, 1), device_id_type=MESH)
        pl.semaphore_signal(barrier, inc=1, device_id=self.sibling(), device_id_type=MESH)
        pl.semaphore_wait(barrier, 10)


def remote(src, dst, send, recv, device):
    return pltpu.make_async_remote_copy(
        src_ref=src, dst_ref=dst, send_sem=send, recv_sem=recv, device_id=device, device_id_type=MESH
    )


LOW, HIGH = pl.ds(0, DEPTH // 2), pl.ds(DEPTH // 2, DEPTH // 2)


class Gather:
    def __init__(self, place, whole, send, recv, parts=None):
        self.place, self.whole, self.send, self.recv, self.parts = place, whole, send, recv, parts

    def block(self, k):
        return self.whole.at[self.place.plane_at(k) * 2 + self.place.core]

    def copy(self, n, source, target, device):
        return remote(source, target, self.send.at[n], self.recv.at[n], device)

    def depth(self, k):
        at = self.place
        here = self.whole.at[at.batch, at.z]
        source = here if self.parts is None else self.parts.at[at.depth_at(k)]
        return self.copy(k - 1, source, here, at.in_depth(k))

    def plane(self, k):
        return self.copy(2 + k, self.block(0), self.block(0), self.place.in_plane(k))

    def across(self, k):
        half = self.block(k).at[LOW if k == 1 else HIGH]
        return self.copy(4 + k, half, half, self.place.in_plane(3 - k))

    def core(self, k):
        return self.copy(7 + k, self.block(k), self.block(k), self.place.sibling())

    def first(self):
        for k in range(1, 4):
            self.depth(k).start()

    def second(self):
        for k in range(1, 4):
            self.depth(k).wait_recv()
        for k in (1, 2):
            self.plane(k).start()
        self.core(0).start()

    def third(self):
        for k in (1, 2):
            self.plane(k).wait_recv()
            self.across(k).start()
            self.core(k).start()

    def fourth(self):
        for k in (1, 2):
            self.across(k).wait_recv()
        self.core(3).start()

    def finish(self):
        for k in range(4):
            self.core(k).wait_recv()
        for k in range(1, 4):
            self.depth(k).wait_send()
        for k in (1, 2):
            self.plane(k).wait_send()
            self.across(k).wait_send()
        for k in range(4):
            self.core(k).wait_send()


class Spread(Gather):
    def step(self, k, other):
        device = self.place.in_plane(k, other) if k else self.place.sibling()
        return self.copy(2 * k + other + 3 if k else 3, self.block(0), self.block(0), device)

    def steps(self):
        return [self.step(0, 0)] + [self.step(k, other) for k in range(1, 4) for other in range(2)]

    def second(self):
        for k in range(1, 4):
            self.depth(k).wait_recv()
        for copy in self.steps():
            copy.start()

    def finish(self):
        for copy in self.steps():
            copy.wait_recv()
        for k in range(1, 4):
            self.depth(k).wait_send()
        for copy in self.steps():
            copy.wait_send()


class Scatter:
    def __init__(self, place, grad, twin, near, far, along, send, recv):
        self.place, self.grad, self.twin = place, grad, twin
        self.near, self.far, self.along, self.send, self.recv = near, far, along, send, recv
        shape = grad.shape
        if len(shape) == 4:
            self.at = lambda p, c: grad.at[p * 2 + c]
        else:
            self.at = lambda p, c: grad.at[p, c]

    def block(self, k):
        return self.at(self.place.plane_at(k), self.place.core)

    def copy(self, n, source, target, device):
        return remote(source, target, self.send.at[n], self.recv.at[n], device)

    def core(self, p):
        source = self.at(p, 1 - self.place.core)
        return self.copy(p, source, self.twin.at[p], self.place.sibling())

    def plane(self, n):
        k, half = ((1, LOW), (3, LOW), (2, HIGH), (3, HIGH))[n]
        target = self.near.at[n]
        return self.copy(4 + n, self.block(k).at[half], target, self.place.in_plane(1 + n // 2))

    def across(self, n):
        k, half = ((2, LOW), (1, HIGH))[n]
        return self.copy(8 + n, self.block(k).at[half], self.far.at[n], self.place.in_plane(2 - n))

    def depth(self, k):
        source = self.block(0).at[self.place.depth_at(k)]
        return self.copy(9 + k, source, self.along.at[k - 1], self.place.in_depth(k))

    def first(self):
        for p in range(PLANE):
            self.core(p).start()

    def second(self):
        for p in range(PLANE):
            self.core(p).wait_recv()
        own = self.place.core

        def one(p, carry):
            mine = self.at(p, own)
            mine[...] = (mine[...].astype(f32) + self.twin[p].astype(f32)).astype(mine.dtype)
            return carry

        lax.fori_loop(0, PLANE, one, 0)
        for n in range(4):
            self.plane(n).start()

    def third(self):
        for n in range(4):
            self.plane(n).wait_recv()
        for n, (k, base) in enumerate(((2, 0), (1, 2))):
            mine = self.block(k)

            def one(q, carry):
                total = mine[base + q].astype(f32) + self.near[2 * n + 1, q].astype(f32)
                mine[base + q] = total.astype(mine.dtype)
                return carry

            lax.fori_loop(0, 2, one, 0)
            self.across(n).start()

    def fourth(self):
        for n in range(2):
            self.across(n).wait_recv()
        mine = self.block(0)

        def one(i, carry):
            n, q = i // 2, i % 2
            total = mine[i].astype(f32) + self.near[2 * n, q].astype(f32) + self.far[n, q].astype(f32)
            mine[i] = total.astype(mine.dtype)
            return carry

        lax.fori_loop(0, DEPTH, one, 0)
        for k in range(1, 4):
            self.depth(k).start()

    def total(self):
        for k in range(1, 4):
            self.depth(k).wait_recv()
        total = self.block(0)[self.place.z].astype(f32)
        for k in range(3):
            total = total + self.along[k].astype(f32)
        return total

    def finish(self):
        for p in range(PLANE):
            self.core(p).wait_send()
        for n in range(4):
            self.plane(n).wait_send()
        for n in range(2):
            self.across(n).wait_send()
        for k in range(1, 4):
            self.depth(k).wait_send()


def turned(ref, value):
    ref[...] = jnp.zeros_like(ref)
    ref[: value.shape[0], : value.shape[1]] = value
    return ref[...].T


def heads_of(block, h):
    return block[h * HEAD_DIM : (h + 1) * HEAD_DIM]


def only_head(block, h):
    zero = jnp.zeros((HEAD_DIM, block.shape[1]), block.dtype)
    mine = heads_of(block, h)
    return jnp.concatenate([mine, zero] if h % 2 == 0 else [zero, mine], 0)


def pair_of(block, h):
    at = h // 2 * 2 * HEAD_DIM
    return block[:, at : at + 2 * HEAD_DIM]


def mask_parts(tag, pair):
    query, key = tag_rows(tag, pair)
    width = tag.shape[1]
    zero = jnp.zeros((128 - AUG, width), bf16)
    return jnp.concatenate([key, zero], 0).T, jnp.concatenate([query, zero], 0)


class Slots:
    def __init__(self, tag_ref, seq, seq_count):
        self.tag_ref, self.seq, self.count = tag_ref, seq, 8 * seq_count
        self.last_pair = 8 * seq_count

    def tag(self, j):
        wide = self.tag_ref[:, pl.ds(pl.multiple_of(j * SLOT, 128), SLOT + 128)]
        offset = HALO - 8 * self.seq - j
        return pltpu.roll(wide, SLOT + 128 - offset, 1)[:1, :SLOT]

    def tail_tag(self):
        tag = self.tag_ref[:, 2048:2176]
        if self.count < TAIL:
            tag = pltpu.roll(tag, 128 - (TAIL - self.count), 1)
        place = lax.broadcasted_iota(jnp.int32, (1, TAIL), 1)
        return jnp.where(place < self.count, tag[:1, :TAIL], 2 * (2 * self.last_pair + 3))

    def tail(self, ref):
        return jnp.concatenate(
            [ref[t * TILE + 2 * SLOT : (t + 1) * TILE, :] for t in range(TILES)], 0
        )

    def set_tail(self, ref, value):
        for t in range(TILES):
            ref[t * TILE + 2 * SLOT : (t + 1) * TILE, :] = value[t * PIECE : (t + 1) * PIECE]


def halves_of(width):
    step = min(width, 128)
    return [slice(i, i + step) for i in range(0, width, step)]


def pair_stack(values, *rest):
    zero = jnp.zeros_like(values[0])
    left = jnp.concatenate([values[0], zero, *rest], 0)
    right = jnp.concatenate([zero, values[1], *rest], 0)
    return left, right


def forward_block(
    xb, tag, pair, lanes, put, wt_ref, biases, xt_ref, qt_ref, kt_ref, vt_ref, lse_ref, s_ref, a_ref,
    kn_ref, ct_ref,
):
    width = xb.shape[0]
    parts = ((kt_ref, None), (qt_ref, biases[0]), (vt_ref, biases[1]))

    def project(n):
        at = (1, 0, 2)[n]
        p = dot(wt_ref[at * D : (at + 1) * D, :], xb, 1, 1)
        s_ref[2 * n, :, :width] = p[:SLOT]
        s_ref[2 * n + 1, :, :width] = p[SLOT:]

    def keep(n):
        out_ref, bias = parts[n]
        for h in range(HEADS):
            at = h % 4 * HEAD_DIM
            value = s_ref[2 * n + h // 4, at : at + HEAD_DIM, :width]
            rows = slice(h * HEAD_DIM, (h + 1) * HEAD_DIM)
            if bias is not None:
                value = value + bias[rows]
            value = value.astype(bf16)
            if n == 1:
                value = (value.astype(f32) * HEAD_DIM**-0.5).astype(bf16)
            out_ref[rows, lanes] = value

    masks = []

    def turn():
        kn_ref[:width, :] = kt_ref[:, lanes].T
        masks.extend(mask_parts(tag, pair))

    def rows_of(h):
        return slice(h * HEAD_DIM, (h + 1) * HEAD_DIM)

    def scores(p):
        key_mask, query_mask = masks
        left = jnp.concatenate([kn_ref[:width, p * 128 : (p + 1) * 128], key_mask], 1)
        both = pair_stack([qt_ref[rows_of(2 * p + i), lanes] for i in range(2)], query_mask)
        if width % 128 == 0:
            s = dot(left, jnp.concatenate(both, 1), 1, 0)
            s_ref[2 * p], s_ref[2 * p + 1] = s[:, :width], s[:, width:]
        else:
            for i in range(2):
                s_ref[2 * p + i, :width, :width] = dot(left, both[i], 1, 0)

    def weigh(p):
        for h in (2 * p, 2 * p + 1):
            for half in halves_of(width):
                s = s_ref[h, :width, half]
                top = jnp.max(s, axis=0, keepdims=True)
                ex = jnp.exp(s - top)
                total = jnp.sum(ex, axis=0, keepdims=True)
                a_ref[h, :width, half] = (ex * (1.0 / total)).astype(bf16)
                at = pl.ds(pl.multiple_of(lanes.start + half.start, 128), half.stop - half.start)
                lse_ref[h : h + 1, at] = top + jnp.log(total)

    def collect(p):
        for h in (2 * p, 2 * p + 1):
            c = dot(vt_ref[rows_of(h), lanes], a_ref[h, :width, :width], 1, 0)
            ct_ref[rows_of(h), :width] = c.astype(bf16)

    def close():
        xt_ref[:D, lanes] = xb.T
        put(ct_ref[:, :width].T)

    call = functools.partial
    ahead = [
        call(project, 0), call(project, 1), call(keep, 0), turn, call(project, 2), call(keep, 1),
        call(keep, 2),
    ]
    return ahead, (scores, weigh, collect), [close]


def together(*blocks):
    for phases in zip(*(block[0] for block in blocks)):
        for phase in phases:
            phase()
    count = len(blocks)

    def stage(n):
        return lambda i: blocks[i % count][1][n](i // count)

    skewed(HEADS // 2 * count, stage(0), stage(1), stage(2))
    for phases in zip(*(block[2] for block in blocks)):
        for phase in phases:
            phase()


def skewed(count, *stages):
    for i in range(count + len(stages) - 1):
        for n, stage in enumerate(stages):
            if 0 <= i - n < count:
                stage(i - n)


def backward_block(
    dr, c, tag, pair, lanes, wo, qt_ref, kt_ref, vt_ref, lse_ref, dpt_ref, s_ref, da_ref, a_ref,
    ds_ref, kn_ref, vn_ref, dct_ref, ct_ref,
):
    width = dr.shape[0]
    masks = []

    def turn():
        kn_ref[:width, :] = kt_ref[:, lanes].T
        vn_ref[:width, :] = vt_ref[:, lanes].T
        masks.extend(mask_parts(tag, pair))

    def spread():
        dct_ref[:, :width] = dot(wo, dr, 1, 1).astype(bf16)
        ct_ref[:, :width] = c.T

    def rows_of(h):
        return slice(h * HEAD_DIM, (h + 1) * HEAD_DIM)

    def scores(p):
        at = slice(p * 128, (p + 1) * 128)
        key_mask, query_mask = masks
        left = jnp.concatenate([kn_ref[:width, at], key_mask], 1)
        both = pair_stack([qt_ref[rows_of(2 * p + i), lanes] for i in range(2)], query_mask)
        both_d = pair_stack([dct_ref[rows_of(2 * p + i), :width] for i in range(2)])
        right = vn_ref[:width, at]
        if width % 128 == 0:
            s = dot(left, jnp.concatenate(both, 1), 1, 0)
            u = 2 * (p % 2)
            s_ref[u], s_ref[u + 1] = s[:, :width], s[:, width:]
            da = dot(right, jnp.concatenate(both_d, 1), 1, 0)
            da_ref[u], da_ref[u + 1] = da[:, :width], da[:, width:]
        else:
            for i in range(2):
                s_ref[2 * (p % 2) + i, :width, :width] = dot(left, both[i], 1, 0)
                da_ref[2 * (p % 2) + i, :width, :width] = dot(right, both_d[i], 1, 0)

    def weigh(p):
        for h in (2 * p, 2 * p + 1):
            rows = rows_of(h)
            for half in halves_of(width):
                at = pl.ds(pl.multiple_of(lanes.start + half.start, 128), half.stop - half.start)
                product = ct_ref[rows, half].astype(f32) * dct_ref[rows, half].astype(f32)
                delta = jnp.sum(product, axis=0, keepdims=True)
                lse = lse_ref[h : h + 1, at]
                for first in range(0, width, 64):
                    keys = slice(first, first + 64)
                    a = jnp.exp(s_ref[h % 4, keys, half] - lse)
                    a_ref[h % 4, keys, half] = a.astype(bf16)
                    ds_ref[h % 4, keys, half] = (a * (da_ref[h % 4, keys, half] - delta)).astype(bf16)

    def collect(p):
        for h in (2 * p, 2 * p + 1):
            rows = rows_of(h)
            ds = ds_ref[h % 4, :width, :width]
            dv = dot(dct_ref[rows, :width], a_ref[h % 4, :width, :width], 1, 1)
            dk = dot(qt_ref[rows, lanes], ds, 1, 1)
            dq = dot(kt_ref[rows, lanes], ds, 1, 0) * HEAD_DIM**-0.5
            dpt_ref[rows, lanes] = dq.astype(bf16)
            dpt_ref[slice(D + rows.start, D + rows.stop), lanes] = dk.astype(bf16)
            dpt_ref[slice(2 * D + rows.start, 2 * D + rows.stop), lanes] = dv.astype(bf16)

    return [turn, spread], (scores, weigh, collect), []


def mean(v):
    return jnp.mean(v, axis=-1, keepdims=True)


def row_sum(v):
    return jnp.sum(v, axis=0, keepdims=True)


def flat(value):
    return value.reshape(-1, value.shape[-1])


BLOCK = 48
MAIN = 2 * SLOT


def eights(v):
    return jnp.sum(v.reshape(-1, 8, v.shape[-1]), axis=0)


def feed_tile(
    t, xs_ref, c_ref, es_ref, wo_ref, w1_ref, w2_ref, vec_ref, dh_ref, gvec_ref,
    acc_ref, other_ref, n1_ref, inv_ref, yb_ref, df_ref, u_ref, g_ref, back_ready, tails,
    awo_ref, aw1_ref, aw2_ref,
):
    first = pl.multiple_of(t * TILE, 16)
    rows = pl.ds(first, TILE)
    piece = pl.ds(pl.multiple_of(t * PIECE, 16), PIECE)
    g_tail, du_tail, df_tail, yb_tail = tails
    bo, b2, g1, c1, g2, c2 = (vec_ref[i : i + 1, :] for i in range(2, 8))
    per = FF // D
    blocks = [slice(i, i + BLOCK) for i in range(0, TILE, BLOCK)]

    def at(block):
        return pl.ds(pl.multiple_of(first + block.start, 16), BLOCK)

    acc_ref[...] = dot(c_ref[rows, :], flat(wo_ref[...]), 1, 0)
    for block in blocks:
        h1 = xs_ref[at(block), :].astype(f32) + (acc_ref[block, :] + bo)
        mid = h1 - mean(h1)
        inv1 = lax.rsqrt(mean(mid * mid) + norm_epsilon)
        n1 = mid * inv1
        n1_ref[block, :] = n1
        inv_ref[block, :] = jnp.broadcast_to(inv1, (BLOCK, 128))
        yb_ref[block, :] = (n1 * g1 + c1).astype(bf16)

    pads = (acc_ref, other_ref)

    def w2_part(k):
        return flat(w2_ref[8 // per * k : 8 // per * (k + 1)])

    def w1_part(k):
        return flat(w1_ref[:, :, :, k * D : (k + 1) * D])

    def up(k):
        pads[k % 2][...] = dot(yb_ref[...], w1_part(k), 1, 0)

    def activate(k):
        cols = slice(k * D, (k + 1) * D)
        b1 = vec_ref[8 + k : 9 + k, :]
        for block in blocks:
            u = pads[k % 2][block, :] + b1
            cdf = 0.5 + 0.5 * lax.erf(u * 0.7071067811865476)
            g_ref[k * TILE + block.start : k * TILE + block.stop, :] = (u * cdf).astype(bf16)
            bell = jnp.exp2(u * u * (-0.5 * math.log2(math.e)) - 0.5 * math.log2(2.0 * math.pi))
            u_ref[block, cols] = cdf + u * bell

    def down(k):
        part = dot(g_ref[k * TILE : (k + 1) * TILE, :], w2_part(k), 1, 0)
        if k == 0:
            dh_ref[rows, :] = part
        else:
            dh_ref[rows, :] += part

    up(0)
    up(1)
    activate(0)
    pl.when(t == 0)(back_ready)
    for k in range(per):
        if k + 2 < per:
            up(k + 2)
        down(k)
        if k + 1 < per:
            activate(k + 1)
    sums = [jnp.zeros((8, D), f32)] * 3
    for block in blocks:
        h2 = (n1_ref[block, :] * g1 + c1) + (dh_ref[at(block), :] + b2)
        mid2 = h2 - mean(h2)
        inv2 = lax.rsqrt(mean(mid2 * mid2) + norm_epsilon)
        n2 = mid2 * inv2
        xs_ref[at(block), :] = (n2 * g2 + c2).astype(bf16)
        e = es_ref[at(block), :].astype(f32)
        en = e * n2
        eg = e * g2
        dh2 = (eg - mean(eg) - n2 * mean(eg * n2)) * inv2
        dh_ref[at(block), :] = dh2
        df = dh2.astype(bf16)
        df_ref[block, :] = df
        sums = [sums[0] + eights(e), sums[1] + eights(en), sums[2] + eights(df.astype(f32))]
    for i, value in zip((7, 6, 3), sums):
        gvec_ref[i : i + 1, :] += row_sum(value)
    dft = df_ref[:MAIN, :].T
    ybt = yb_ref[:MAIN, :].T
    df_tail[piece, :] = df_ref[MAIN:, :]
    yb_tail[piece, :] = yb_ref[MAIN:, :]

    def up_back(k):
        pads[k % 2][...] = dot(df_ref[...], w2_part(k), 1, 1)

    def activate_back(k):
        cols = slice(k * D, (k + 1) * D)
        here = slice(k * TILE, k * TILE + MAIN)
        at_tail = pl.ds(pl.multiple_of(k * TAIL + t * PIECE, 16), PIECE)
        aw2_ref[:, cols] += dot(dft, g_ref[here, :], 1, 0)
        g_tail[at_tail, :] = g_ref[here.stop : here.stop + PIECE, :]
        total = jnp.zeros((8, D), f32)
        for block in blocks:
            du = (pads[k % 2][block, :] * u_ref[block, cols]).astype(bf16)
            g_ref[k * TILE + block.start : k * TILE + block.stop, :] = du
            total = total + eights(du.astype(f32))
        gvec_ref[8 + k : 9 + k, :] += row_sum(total)

    def down_back(k):
        cols = slice(k * D, (k + 1) * D)
        here = slice(k * TILE, k * TILE + MAIN)
        at_tail = pl.ds(pl.multiple_of(k * TAIL + t * PIECE, 16), PIECE)
        aw1_ref[:, cols] += dot(ybt, g_ref[here, :], 1, 0)
        du_tail[at_tail, :] = g_ref[here.stop : here.stop + PIECE, :]
        part = dot(g_ref[k * TILE : (k + 1) * TILE, :], w1_part(k), 1, 1)
        dh_ref[rows, :] += part

    skewed(per, up_back, activate_back, down_back)
    sums = [jnp.zeros((8, D), f32)] * 3
    for block in blocks:
        dy = dh_ref[at(block), :]
        n1 = n1_ref[block, :]
        eg = dy * g1
        dh1 = (eg - mean(eg) - n1 * mean(eg * n1)) * inv_ref[block, :1]
        dh_ref[at(block), :] = dh1
        dr = dh1.astype(bf16)
        es_ref[at(block), :] = dr
        sums = [sums[0] + eights(dy), sums[1] + eights(dy * n1), sums[2] + eights(dr.astype(f32))]
    for i, value in zip((5, 4, 2), sums):
        gvec_ref[i : i + 1, :] += row_sum(value)
    main = pl.ds(first, MAIN)
    awo_ref[...] += dot(c_ref[main, :].T, es_ref[main, :], 1, 0)


def whole_kernel(*refs):
    refs = list(refs)

    def take(count):
        taken = refs[:count]
        del refs[:count]
        return taken

    state_in = take(15)
    tok_ref, cot_ref, seg_ref, keep_ref = take(4)
    out_ref, in_ref = take(2)
    state_out = take(5)
    copy_out = take(5)
    out_back, in_back = take(2)
    packed = take(5)
    firsts, seconds, masters = ([p.at[n] for p in packed] for n in range(3))
    state = masters + firsts + seconds
    weights = take(5)
    wa_ref, wo_ref, w1_ref, w2_ref, wv_ref = weights
    xs_ref, es_ref, xt_ref, qt_ref, kt_ref, vt_ref, c_ref, lse_ref, dh_ref, tag_ref = take(10)
    ext_ref, seg_halo, keep_halo = take(3)
    square, gvec_ref, gwa_ref, gwo_ref, grad_vec, halo_out, halo_in = take(7)
    twins, nears, fars, alongs = take(5), take(5), take(5), take(5)
    parts, copies, whole_vec = take(4), take(5), take(1)[0]
    (
        state_sems, load_sems, gather_send, gather_recv, edge_send, edge_recv,
        sum_send, sum_recv, copy_send, copy_recv, store_sems,
    ) = refs
    place = Place()
    seq, seq_count = place.z, DEPTH
    is_last = seq == seq_count - 1
    slots = Slots(tag_ref, seq, seq_count)
    rows = tok_ref.shape[1]
    ext_x, ext_e = ext_ref.at[pl.ds(0, HALO + rows)], ext_ref.at[pl.ds(HALO + rows, HALO + rows)]

    loads = [pltpu.make_async_copy(state_in[i], state[i], state_sems.at[i]) for i in range(15)]
    for load in loads:
        load.start()
    big_loads = [
        pltpu.make_async_copy(src.at[0], dst.at[pl.ds(HALO, rows)], load_sems.at[i])
        for i, (src, dst) in enumerate(((tok_ref, ext_x), (cot_ref, ext_e)))
    ]
    for load in big_loads:
        load.start()
    place.greet()
    edge = [
        remote(src, dst, edge_send.at[i], edge_recv.at[i], place.in_depth(1))
        for i, (src, dst) in enumerate((
            (tok_ref.at[0, pl.ds(rows - HALO, HALO)], ext_x.at[pl.ds(0, HALO)]),
            (cot_ref.at[0, pl.ds(rows - HALO, HALO)], ext_e.at[pl.ds(0, HALO)]),
            (seg_ref.at[:, pl.ds(rows - 128, 128)], seg_halo),
            (keep_ref.at[:, pl.ds(rows - 128, 128)], keep_halo),
        ))
    ]
    gathers = [Gather(place, weights[i], gather_send.at[i], gather_recv.at[i]) for i in range(5)]

    def put(i):
        shard = turned(square, masters[4][...])[: masters[4].shape[1]] if i == 4 else masters[i][...]
        weights[i][place.batch, place.z] = shard.astype(bf16)

    for i in (0, 4):
        loads[i].wait()
        put(i)
        gathers[i].first()
    for copy in edge:
        copy.start()
    for i in (1, 2, 3):
        loads[i].wait()
        put(i)
    gathers[1].first()
    for load in big_loads:
        load.wait()
    for copy in edge:
        copy.wait()
    tag_ref[...] = jnp.zeros_like(tag_ref)
    rim = seg_halo[...] * 2 + keep_halo[...]
    tag_ref[:, :HALO] = jnp.broadcast_to(rim[:, 128 - HALO :], (8, HALO))
    tag_ref[:, HALO : HALO + rows] = jnp.broadcast_to(seg_ref[...] * 2 + keep_ref[...], (8, rows))

    def stage_one(j, carry):
        start = first_row(j, seq)
        row = slot_row(j)
        stage_slot(ext_x, start, xs_ref, row)
        stage_slot(ext_e, start, es_ref, row)
        return carry

    gathers[0].second()
    gathers[2].first()
    gathers[4].second()
    gathers[1].second()
    lax.fori_loop(0, 8, stage_one, 0)
    slots.set_tail(xs_ref, tail_rows(ext_x, slots.count, is_last))
    slots.set_tail(es_ref, tail_rows(ext_e, slots.count, is_last))
    gathers[0].third()
    gathers[4].third()
    xt_ref[:, 8 * SLOT :] = jnp.zeros((D + AUG, 128), bf16)
    ones = lax.broadcasted_iota(jnp.int32, (AUG, LANES), 0) == 0
    xt_ref[D:, :] = jnp.where(ones, 1.0, 0.0).astype(bf16)
    gathers[2].second()
    gathers[3].first()
    gathers[0].fourth()
    gathers[4].fourth()
    gathers[1].third()
    gathers[0].finish()
    gathers[4].finish()
    gathers[3].second()

    def forward(wt_ref, s_ref, a_ref, kn_ref, ct_ref):
        for part in range(3):
            wt_ref[part * D : (part + 1) * D, :] = flat(
                wa_ref[:, :, :, part * D : (part + 1) * D]
            ).T
        vec_t = flat(wv_ref[...])
        biases = (vec_t[:, 0:1].astype(f32), vec_t[:, 1:2].astype(f32))

        def block(n, xb, tag, pair, lanes, put):
            return forward_block(
                xb, tag, pair, lanes, put, wt_ref, biases, xt_ref, qt_ref, kt_ref, vt_ref, lse_ref,
                s_ref.at[n], a_ref.at[n], kn_ref.at[n], ct_ref.at[n],
            )

        def two(i, carry):
            for step, event in (
                (1, gathers[1].fourth), (1, gathers[2].third), (3, gathers[2].fourth),
                (3, gathers[3].third),
            ):
                pl.when(i == step)(event)

            def slot(n):
                j = 2 * i + n
                at = pl.ds(slot_row(j), SLOT)
                lanes = pl.ds(pl.multiple_of(j * SLOT, 128), SLOT)

                def put(value):
                    c_ref[at, :] = value

                return block(n, xs_ref[at, :], slots.tag(j), 8 * seq + j, lanes, put)

            together(slot(0), slot(1))
            return carry

        lax.fori_loop(0, 4, two, 0)
        together(
            block(
                0, slots.tail(xs_ref), slots.tail_tag(), slots.last_pair, pl.ds(8 * SLOT, TAIL),
                functools.partial(slots.set_tail, c_ref),
            )
        )

    pl.run_scoped(
        forward,
        pltpu.VMEM((3 * D, D), bf16),
        pltpu.VMEM((2, HEADS, SLOT, SLOT), f32),
        pltpu.VMEM((2, HEADS, SLOT, SLOT), bf16),
        pltpu.VMEM((2, SLOT, D), bf16),
        pltpu.VMEM((2, D, SLOT), bf16),
    )
    for i in (1, 2):
        gathers[i].finish()
    gathers[3].fourth()

    def back_ready():
        gathers[3].finish()

    grads = [gwa_ref, gwo_ref, w1_ref, w2_ref, grad_vec]
    scatters = [
        Scatter(
            place, grads[i], twins[i], nears[i], fars[i], alongs[i], sum_send.at[i], sum_recv.at[i]
        )
        for i in range(5)
    ]

    def feed_all(
        vec_ref, acc_ref, other_ref, n1_ref, inv_ref, u_ref, awo_ref, aw1_ref, aw2_ref
    ):
        used = 0
        views = []
        for count in (4 * TILE, TILE, TILE, TAIL, TAIL, 4 * TAIL, 4 * TAIL):
            views.append(ext_ref.at[pl.ds(used, count)])
            used += count
        g_ref, yb_ref, df_ref, yb_tail, df_tail, g_tail, du_tail = views
        for ref in (awo_ref, aw1_ref, aw2_ref, gvec_ref):
            ref[...] = jnp.zeros_like(ref)
        vec_ref[...] = flat(wv_ref[...]).astype(f32).T[:16]

        def one(t, carry):
            feed_tile(
                t, xs_ref, c_ref, es_ref, wo_ref, w1_ref, w2_ref, vec_ref, dh_ref, gvec_ref, acc_ref,
                other_ref, n1_ref, inv_ref, yb_ref, df_ref, u_ref, g_ref, back_ready,
                (g_tail, du_tail, df_tail, yb_tail),
                awo_ref, aw1_ref, aw2_ref,
            )
            return carry

        lax.fori_loop(0, TILES, one, 0)
        for k in range(FF // D):
            cols = slice(k * D, (k + 1) * D)
            at = slice(k * TAIL, (k + 1) * TAIL)
            aw2_ref[:, cols] += dot(df_tail[...].T, g_tail[at, :], 1, 0)
            aw1_ref[:, cols] += dot(yb_tail[...].T, du_tail[at, :], 1, 0)
        awo_ref[...] += dot(slots.tail(c_ref).T, slots.tail(es_ref), 1, 0)
        def convert(i, carry):
            value = aw2_ref[:, pl.ds(pl.multiple_of(i * 128, 128), 128)].astype(bf16).T
            w2_ref[i // 2, pl.ds(i % 2 * 2, 2)] = value.reshape(2, -1, D)
            return carry

        def convert_rows(i, carry):
            value = aw1_ref[pl.ds(pl.multiple_of(i * 64, 64), 64), :].astype(bf16)
            w1_ref[i] = value.reshape(DEPTH, -1, FF)
            gwo_ref[i // 2, i % 2] = (
                awo_ref[pl.ds(pl.multiple_of(i * 64, 64), 64), :].astype(bf16).reshape(DEPTH, -1, D)
            )
            return carry

        lax.fori_loop(0, FF // 128, convert, 0)
        scatters[3].first()
        lax.fori_loop(0, 8, convert_rows, 0)
        scatters[2].first()
        scatters[1].first()

    pl.run_scoped(
        feed_all,
        pltpu.VMEM((16, D), f32),
        pltpu.VMEM((TILE, D), f32),
        pltpu.VMEM((TILE, D), f32),
        pltpu.VMEM((TILE, D), f32),
        pltpu.VMEM((TILE, 128), f32),
        pltpu.VMEM((TILE, FF), f32),
        pltpu.VMEM((D, D), f32),
        pltpu.VMEM((D, FF), f32),
        pltpu.VMEM((D, FF), f32),
    )
    for load in loads[5:]:
        load.wait()
    copy_gathers = [
        kind(place, copies[i], copy_send.at[i], copy_recv.at[i], parts[i])
        for i, kind in enumerate((Spread, Spread, Gather, Gather))
    ]
    copy_gathers.append(Spread(place, whole_vec, copy_send.at[4], copy_recv.at[4]))
    stores = []

    def store(src, dst):
        stores.append(pltpu.make_async_copy(src, dst, store_sems.at[len(stores)]))
        stores[-1].start()

    def update(i):
        total = scatters[i].total()
        if i == 4:
            square[...] = jnp.zeros_like(square)
            square[: total.shape[0], :] = total
            here, cols = masters[4].shape
            total = square[...].T[:here, :cols]
        new = adam_update(masters[i][...], firsts[i][...], seconds[i][...], total, learn_rates[i])
        firsts[i][...], seconds[i][...], masters[i][...] = new
        if i == 4:
            shard = turned(square, new[2])[: new[2].shape[1]].astype(bf16)
            whole_vec[place.batch, place.z] = shard
        else:
            low = new[2].astype(bf16)
            width = low.shape[1] // DEPTH
            for q in range(DEPTH):
                parts[i][q] = low[:, q * width : (q + 1) * width]
            copies[i][place.batch, place.z] = parts[i][place.z]
        copy_gathers[i].first()

    def backward(dpt_ref):
        dpt_ref[:, 8 * SLOT :] = jnp.zeros((3 * D, 128), bf16)

        def attention(s_ref, da_ref, a_ref, ds_ref, kn_ref, vn_ref, dct_ref, ct_ref):
            wo = flat(wo_ref[...])
            pads = (s_ref, da_ref, a_ref, ds_ref, kn_ref, vn_ref, dct_ref, ct_ref)

            def block(n, dr, c, tag, pair, lanes):
                return backward_block(
                    dr, c, tag, pair, lanes, wo, qt_ref, kt_ref, vt_ref, lse_ref, dpt_ref,
                    *(pad.at[n] for pad in pads),
                )

            def two(i, carry):
                for step, event in (
                    (1, scatters[3].second), (1, scatters[2].second), (3, scatters[3].third),
                    (3, scatters[1].second),
                ):
                    pl.when(i == step)(event)

                def slot(n):
                    j = 2 * i + n
                    at = pl.ds(slot_row(j), SLOT)
                    lanes = pl.ds(pl.multiple_of(j * SLOT, 128), SLOT)
                    return block(n, es_ref[at, :], c_ref[at, :], slots.tag(j), 8 * seq + j, lanes)

                together(slot(0), slot(1))
                return carry

            lax.fori_loop(0, 4, two, 0)
            together(
                block(
                    0, slots.tail(es_ref), slots.tail(c_ref), slots.tail_tag(), slots.last_pair,
                    pl.ds(8 * SLOT, TAIL),
                )
            )

        pl.run_scoped(
            attention,
            *[pltpu.VMEM((2, 4, SLOT, SLOT), f32)] * 2,
            *[pltpu.VMEM((2, 4, SLOT, SLOT), bf16)] * 2,
            *[pltpu.VMEM((2, SLOT, D), bf16)] * 2,
            *[pltpu.VMEM((2, D, SLOT), bf16)] * 2,
        )
        pl.run_scoped(
            functools.partial(finish, dpt_ref),
            pltpu.VMEM((HALO + rows + 16, D), f32),
            pltpu.VMEM((4, SLOT, SLOT), f32),
        )

    def finish(dpt_ref, ext_ref, s_ref):
        low_ref = ext_e
        for part in range(3):
            cols = slice(part * D, (part + 1) * D)
            g = dot(xt_ref[...], dpt_ref[cols, :], 1, 1)
            gwa_ref[:, :, :, :, cols] = g[:D].astype(bf16).reshape(PLANE, 2, DEPTH, -1, D)
            if part != 1:
                gvec_ref[part // 2 : part // 2 + 1, :] = g[D : D + 1]
        grad_vec[...] = gvec_ref[...].T.reshape(grad_vec.shape)
        scatters[0].first()
        scatters[4].first()
        scatters[2].third()

        def output_one(j, carry):
            at = pl.ds(slot_row(j), SLOT)
            unstage_slot(
                ext_ref, first_row(j, seq),
                lambda g: xs_ref[at, g * 128 : (g + 1) * 128].astype(f32),
            )
            return carry

        def close(value):
            @pl.when(is_last)
            def _():
                ext_ref[HALO + rows - slots.count : HALO + rows, :] = value[: slots.count]

        lax.fori_loop(0, 8, output_one, 0)
        close(slots.tail(xs_ref).astype(f32))
        scatters[0].second()
        scatters[4].second()
        scatters[3].fourth()
        scatters[1].third()
        low_ref[...] = ext_ref[: HALO + rows, :].astype(bf16)
        halo_out[...] = low_ref[:HALO, :]
        edge_back[0].start()
        store(low_ref.at[pl.ds(HALO, rows)], out_ref)
        wa = flat(wa_ref[...])

        def input_block(lanes):
            return dot(wa, dpt_ref[:, lanes], 1, 0).T

        def input_two(i, carry):
            for step, event in (
                (1, scatters[2].fourth), (2, scatters[1].fourth), (2, functools.partial(update, 3)),
                (3, scatters[0].third), (3, scatters[4].third),
            ):
                pl.when(i == step)(event)

            def product(n):
                lanes = pl.ds(pl.multiple_of((2 * i + n) * SLOT, 128), SLOT)
                grad = dot(wa, dpt_ref[:, lanes], 1, 0)
                s_ref[2 * n], s_ref[2 * n + 1] = grad[:SLOT], grad[SLOT:]

            def put_back(n):
                j = 2 * i + n
                at = pl.ds(slot_row(j), SLOT)

                def column(g):
                    part = s_ref[2 * n + g // 2, g % 2 * 128 : g % 2 * 128 + 128, :].T
                    return part + dh_ref[at, g * 128 : (g + 1) * 128]

                unstage_slot(ext_ref, first_row(j, seq), column)

            skewed(2, product, put_back)
            return carry

        lax.fori_loop(0, 4, input_two, 0)
        close(input_block(pl.ds(8 * SLOT, TAIL)) + slots.tail(dh_ref))
        halo_in[...] = ext_ref[:HALO, :]
        edge_back[1].start()
        store(ext_ref.at[pl.ds(HALO, rows)], in_ref)
        update(2)
        copy_gathers[3].second()
        scatters[0].fourth()
        scatters[4].fourth()
        update(1)
        copy_gathers[2].second()
        update(4)
        update(0)
        copy_gathers[3].third()
        copy_gathers[2].third()
        copy_gathers[1].second()
        copy_gathers[4].second()
        copy_gathers[0].second()
        copy_gathers[3].fourth()
        copy_gathers[2].fourth()
        for i in range(5):
            store(packed[i], state_out[i])
        for i in (3, 2, 1, 4, 0):
            copy_gathers[i].finish()
            scatters[i].finish()
        here = masters[4].shape[0]
        mine = jnp.concatenate([whole_vec[seq * 2 + q // 4, q % 4] for q in range(8)], 0)
        copies[4][...] = mine.astype(f32).T[:here].astype(bf16)
        for i in range(5):
            store(copies[i], copy_out[i])
        for copy in stores:
            copy.wait()
        for copy in edge_back:
            copy.wait()

    edge_back = [
        remote(halo_out, out_back, edge_send.at[4], edge_recv.at[4], place.in_depth(3)),
        remote(halo_in, in_back, edge_send.at[5], edge_recv.at[5], place.in_depth(3)),
    ]
    pl.run_scoped(backward, pltpu.VMEM((3 * D, LANES), bf16))


def whole(masters, firsts, seconds, tokens, cotangent, segment, keep):
    shape = jax.ShapeDtypeStruct
    vmem = pl.BlockSpec(memory_space=pltpu.VMEM)
    hbm = pl.BlockSpec(memory_space=pl.ANY)
    state = (*masters, *firsts, *seconds)
    rows = tokens.shape[1]
    r = masters[0].shape[0]
    shapes = ((r, 3 * D), (r, D), (r, FF), (4 * r, D))
    copies = [((8, DEPTH, s[0], s[1] // DEPTH), bf16) for s in shapes]
    copies.append(((masters[4].shape[0], 128), bf16))
    halos = [((HALO, D), bf16), ((HALO, D), f32)]
    out_shape = [
        shape((rows, D), bf16),
        shape((rows, D), f32),
        *[shape((3,) + s.shape, f32) for s in masters],
        *[shape(*c) for c in copies],
        *[shape(*h) for h in halos],
    ]
    five = [(s, bf16) for s in shapes] + [((r, 128), f32)]
    tall = ROWS
    scratch = [pltpu.VMEM((3,) + s.shape, f32) for s in masters]
    scratch += [pltpu.VMEM((8, DEPTH) + s, bf16) for s in (*shapes, (r, 128))]
    scratch += [
        pltpu.VMEM((tall, D), bf16),
        pltpu.VMEM((tall, D), bf16),
        pltpu.VMEM((D + AUG, LANES), bf16),
        pltpu.VMEM((D, LANES), bf16),
        pltpu.VMEM((D, LANES), bf16),
        pltpu.VMEM((D, LANES), bf16),
        pltpu.VMEM((tall, D), bf16),
        pltpu.VMEM((HEADS, LANES), f32),
        pltpu.VMEM((tall, D), f32),
        pltpu.VMEM((8, LANES), jnp.int32),
        pltpu.VMEM((2 * (HALO + rows), D), bf16),
        pltpu.VMEM((1, 128), jnp.int32),
        pltpu.VMEM((1, 128), jnp.int32),
        pltpu.VMEM((128, 128), f32),
        pltpu.VMEM((128, D), f32),
        pltpu.VMEM((PLANE, 2, DEPTH) + shapes[0], bf16),
        pltpu.VMEM((PLANE, 2, DEPTH) + shapes[1], bf16),
        pltpu.VMEM((PLANE, 2, DEPTH, r, 128), f32),
        *[pltpu.VMEM(*h) for h in halos],
    ]
    for lead in ((PLANE, DEPTH), (4, DEPTH // 2), (2, DEPTH // 2), (3,)):
        scratch += [pltpu.VMEM(lead + s, t) for s, t in five]
    scratch += [pltpu.VMEM((DEPTH, s[0], s[1] // DEPTH), bf16) for s in shapes]
    scratch += [pltpu.VMEM(*c) for c in copies]
    scratch.append(pltpu.VMEM((8, DEPTH, r, 128), bf16))
    dma = pltpu.SemaphoreType.DMA
    scratch += [
        dma((15,)), dma((2,)), dma((5, 11)), dma((5, 11)), dma((6,)), dma((6,)),
        dma((5, 13)), dma((5, 13)), dma((5, 11)), dma((5, 11)), dma((12,)),
    ]
    return pl.pallas_call(
        whole_kernel,
        out_shape=out_shape,
        in_specs=[hbm] * 17 + [vmem] * 2,
        out_specs=[hbm] * 12 + [vmem] * 2,
        scratch_shapes=scratch,
        compiler_params=pltpu.CompilerParams(
            collective_id=0, has_side_effects=True, vmem_limit_bytes=63 * MIB
        ),
        name="whole",
    )(*state, tokens, cotangent, segment, keep)


LAST_PART = 496


def last_kernel(*refs):
    results, backs, ends = refs[:12], refs[12:14], refs[14:36]
    lows, (load_sems, store_sems) = refs[36:48], refs[48:]
    rows = results[0].shape[0]
    seq = lax.axis_index("seq")
    rim = pl.ds(rows - HALO, HALO)
    places = [(i, rim) for i in range(2)]
    places += [
        (i, pl.ds(first, LAST_PART))
        for i in (1, 0)
        for first in range(0, rows - HALO, LAST_PART)
    ]
    places += [(i, pl.ds(0, results[i].shape[0])) for i in range(2, 12)]
    loads = [
        pltpu.make_async_copy(results[i].at[at], lows[i].at[at], load_sems.at[n])
        for n, (i, at) in enumerate(places)
    ]
    for load in loads:
        load.start()
    place = lax.broadcasted_iota(jnp.int32, (HALO, 1), 0)
    theirs = (place >= HALO - 8 * (seq + 1)) & (seq < lax.axis_size("seq") - 1)
    stores = []
    for n, (i, at) in enumerate(places):
        loads[n].wait()
        if n < 2:
            own = lows[i][rim, :].astype(f32)
            lows[i][rim, :] = jnp.where(theirs, backs[i][...].astype(f32), own).astype(lows[i].dtype)
        if i < 2:
            pairs = [(lows[i].at[at], ends[i].at[at])]
        elif i < 7:
            pairs = [(lows[i].at[part], ends[2 + 5 * part + i - 2]) for part in range(3)]
        else:
            pairs = [(lows[i], ends[10 + i])]
        for source, target in pairs:
            stores.append(pltpu.make_async_copy(source, target, store_sems.at[len(stores)]))
            stores[-1].start()
    for store in stores:
        store.wait()


def last(results, out_back, in_back):
    shape = jax.ShapeDtypeStruct
    vmem = pl.BlockSpec(memory_space=pltpu.VMEM)
    hbm = pl.BlockSpec(memory_space=pl.ANY)
    loads = 12 + 2 * ((results[0].shape[0] - HALO) // LAST_PART)
    ends = list(results[:2])
    for part in range(3):
        ends += [shape(a.shape[1:], a.dtype) for a in results[2:7]]
    ends += results[7:]
    return pl.pallas_call(
        last_kernel,
        out_shape=[shape(a.shape, a.dtype) for a in ends],
        in_specs=[hbm] * 12 + [vmem, vmem],
        out_specs=[hbm] * 22,
        scratch_shapes=[pltpu.VMEM(a.shape, a.dtype) for a in results]
        + [pltpu.SemaphoreType.DMA((loads,)), pltpu.SemaphoreType.DMA((loads + 10,))],
        compiler_params=pltpu.CompilerParams(vmem_limit_bytes=60 * MIB),
        name="last",
    )(*results, out_back, in_back)


def on_device(
    tokens,
    cotangent,
    segment,
    keep_mask,
    attn_master,
    out_master,
    in_master,
    back_master,
    vec_master,
    attn_first,
    out_first,
    in_first,
    back_first,
    vec_first,
    attn_second,
    out_second,
    in_second,
    back_second,
    vec_second,
):
    seq = lax.axis_index("seq")
    seq_count = lax.axis_size("seq")
    both = ("batch", "seq")
    rows = tokens.shape[1]
    masters = (attn_master, out_master, in_master, back_master, vec_master)
    firsts = (attn_first, out_first, in_first, back_first, vec_first)
    seconds = (attn_second, out_second, in_second, back_second, vec_second)
    direct = seq_count == DEPTH and lax.axis_size("batch") == 2 * PLANE
    forward = [(i, i + 1) for i in range(seq_count - 1)]
    backward = [(i + 1, i) for i in range(seq_count - 1)]
    if direct:
        *results, out_back, grad_back = whole(
            masters, firsts, seconds, tokens, cotangent, segment, keep_mask
        )
        for i in range(7, 11):
            results[i] = results[i].reshape(-1, results[i].shape[-1])
        ends = last(results, out_back, grad_back)
        return (ends[0][None], ends[1][None], *ends[2:])
    low = [w.astype(bf16) for w in masters]
    low[4] = jnp.pad(low[4].T, ((0, 0), (0, 128 - low[4].shape[0])))
    attn_w, out_w, in_w, back_w, vec_t = (
        lax.all_gather(w, both, axis=0, tiled=True) for w in low
    )
    x_halo, e_halo, seg_halo, keep_halo = (
        lax.ppermute(a, "seq", forward)
        for a in (
            tokens[0, rows - HALO :], cotangent[0, rows - HALO :],
            segment[:, rows - 128 :], keep_mask[:, rows - 128 :],
        )
    )
    xs, es, xt, qt, kt, vt, c, lse = attn_forward(
        seq_count, tokens, cotangent, x_halo, e_halo, segment, keep_mask, seg_halo, keep_halo,
        attn_w, vec_t,
    )
    z, dh, dr, gwo, gw1, gw2, gvec, gb1 = feed(xs, c, es, out_w, in_w, back_w, vec_t)
    out, out_halo, grad_in, grad_in_halo, gwa, gbias = attn_backward(
        seq_count, xt, qt, kt, vt, lse, dr, dh, z, attn_w, out_w
    )
    grads = (gwa, gwo, gw1, gw2)
    grad_vec = jnp.concatenate(
        [gbias[:1, :D], gbias[:1, 2 * D :], gvec[2:8], gb1[0].reshape(FF // D, D)], 0
    )
    sums = [lax.psum_scatter(g.astype(f32), both, scatter_dimension=0, tiled=True) for g in grads]
    sums.append(lax.psum_scatter(grad_vec, both, scatter_dimension=1, tiled=True))
    new = [
        adam_update(masters[i], firsts[i], seconds[i], sums[i], learn_rates[i]) for i in range(5)
    ]

    def own_columns(i):
        whole = lax.all_gather(new[i][2].astype(bf16), both, axis=1 if i == 4 else 0, tiled=True)
        count = whole.shape[1] // seq_count
        return lax.dynamic_slice_in_dim(whole, seq * count, count, 1)

    results = [out, grad_in] + [jnp.stack(new[i]) for i in range(5)]
    results += [own_columns(i) for i in range(5)]
    out_back = lax.ppermute(out_halo, "seq", backward)
    grad_back = lax.ppermute(grad_in_halo, "seq", backward)
    ends = last(results, out_back, grad_back)
    return (ends[0][None], ends[1][None], *ends[2:])


def solution(mesh):
    stream = P("batch", "seq", None)
    rows = P(("batch", "seq"), None)
    vector = P(None, ("batch", "seq"))
    five = (rows, rows, rows, rows, vector)
    return jax.shard_map(
        on_device,
        mesh=mesh,
        in_specs=(stream, stream, P("batch", "seq"), P("batch", "seq")) + five * 3,
        out_specs=(stream, stream) + five * 3 + (P(None, "seq"),) * 5,
        check_vma=False,
    )
```

profile of v0, /device:TPU:0, one launch (start us, length us, event | category | flops | bytes accessed | tf_op | source)
XLA Modules:
  0.0 183.1 jit_solution(13322529197975440294)
XLA Ops:
  0.7 173.9 %whole.1 = (bf16[2048,512]{1,0:T(8,128)(2,1)}, f32[2048,512]{1,0:T(8,128)}, f32[3,16,1536]{2,1,0:T(8,128)}, f32[3,16,512]{2,1,0:T(8,128)}, f32[3,16,2048]{2,1,0:...) custom-call(f32[16,1536]{1,0:T(8,128)} %refs_0_.1, ...), custom_call_target="tpu_custom_call" | custom-call | tf_op jit(solution)/shard_map/whole/pallas_call | solution.py:1551
  174.6 8.3 %last.1 = (bf16[2048,512]{1,0:T(8,128)(2,1)}, f32[2048,512]{1,0:T(8,128)}, f32[16,1536]{1,0:T(8,128)}, f32[16,512]{1,0:T(8,128)}, f32[16,2048]{1,0:T(8,128)}, /*...) custom-call(bf16[2048,512]{1,0:T(8,128)(2,1)} %get-tuple-element.58., ...), custom_call_target="tpu_custom_call" | custom-call | tf_op jit(solution)/shard_map/last/pallas_call | solution.py:1616
where the time goes:
time: 183 us
  Pallas kernels  182 us (99%)
    pallas_call x1, Pallas kernels, whole(): pl.pallas_call(whole_kernel, out_shape=out_shape, in_specs=[hbm] * 17 + [...  174 us
    pallas_call x1, Pallas kernels, last(): pl.pallas_call(last_kernel, out_shape=[shape(a.shape, a.dtype) for a in e...  8.32 us

commit v1 on v0

--- a/solution.py
+++ b/solution.py
@@ -53,6 +53,8 @@
 
 
 def slot_row(j):
+    if isinstance(j, int):
+        return (j // 2) * TILE + (j % 2) * SLOT
     return pl.multiple_of((j // 2) * TILE + (j % 2) * SLOT, 16)
 
 
@@ -502,7 +504,9 @@
             pl.semaphore_signal(barrier, inc=1, device_id=self.in_depth(k), device_id_type=MESH)
             pl.semaphore_signal(barrier, inc=1, device_id=self.in_plane(k, 1), device_id_type=MESH)
         pl.semaphore_signal(barrier, inc=1, device_id=self.sibling(), device_id_type=MESH)
-        pl.semaphore_wait(barrier, 10)
+
+    def greeted(self):
+        pl.semaphore_wait(pltpu.get_barrier_semaphore(), 10)
 
 
 def remote(src, dst, send, recv, device):
@@ -730,7 +734,7 @@
         self.last_pair = 8 * seq_count
 
     def tag(self, j):
-        wide = self.tag_ref[:, pl.ds(pl.multiple_of(j * SLOT, 128), SLOT + 128)]
+        wide = self.tag_ref[:, pl.ds(lanes_of(j).start, SLOT + 128)]
         offset = HALO - 8 * self.seq - j
         return pltpu.roll(wide, SLOT + 128 - offset, 1)[:1, :SLOT]
 
@@ -749,6 +753,13 @@
     def set_tail(self, ref, value):
         for t in range(TILES):
             ref[t * TILE + 2 * SLOT : (t + 1) * TILE, :] = value[t * PIECE : (t + 1) * PIECE]
+
+
+def part_of(lanes, half):
+    start = lanes.start + half.start
+    if not isinstance(start, int):
+        start = pl.multiple_of(start, 128)
+    return pl.ds(start, half.stop - half.start)
 
 
 def halves_of(width):
@@ -817,7 +828,7 @@
                 ex = jnp.exp(s - top)
                 total = jnp.sum(ex, axis=0, keepdims=True)
                 a_ref[h, :width, half] = (ex * (1.0 / total)).astype(bf16)
-                at = pl.ds(pl.multiple_of(lanes.start + half.start, 128), half.stop - half.start)
+                at = part_of(lanes, half)
                 lse_ref[h : h + 1, at] = top + jnp.log(total)
 
     def collect(p):
@@ -835,6 +846,19 @@
         call(keep, 2),
     ]
     return ahead, (scores, weigh, collect), [close]
+
+
+def when(condition, event):
+    if isinstance(condition, bool):
+        if condition:
+            event()
+    else:
+        pl.when(condition)(event)
+
+
+def lanes_of(j):
+    start = j * SLOT
+    return pl.ds(start if isinstance(j, int) else pl.multiple_of(start, 128), SLOT)
 
 
 def together(*blocks):
@@ -900,7 +924,7 @@
         for h in (2 * p, 2 * p + 1):
             rows = rows_of(h)
             for half in halves_of(width):
-                at = pl.ds(pl.multiple_of(lanes.start + half.start, 128), half.stop - half.start)
+                at = part_of(lanes, half)
                 product = ct_ref[rows, half].astype(f32) * dct_ref[rows, half].astype(f32)
                 delta = jnp.sum(product, axis=0, keepdims=True)
                 lse = lse_ref[h : h + 1, at]
@@ -1101,6 +1125,7 @@
         sum_send, sum_recv, copy_send, copy_recv, store_sems,
     ) = refs
     place = Place()
+    place.greet()
     seq, seq_count = place.z, DEPTH
     is_last = seq == seq_count - 1
     slots = Slots(tag_ref, seq, seq_count)
@@ -1116,7 +1141,7 @@
     ]
     for load in big_loads:
         load.start()
-    place.greet()
+    place.greeted()
     edge = [
         remote(src, dst, edge_send.at[i], edge_recv.at[i], place.in_depth(1))
         for i, (src, dst) in enumerate((
@@ -1193,41 +1218,40 @@
                 s_ref.at[n], a_ref.at[n], kn_ref.at[n], ct_ref.at[n],
             )
 
-        def two(i, carry):
+        def two(i, carry, *more):
             for step, event in (
                 (1, gathers[1].fourth), (1, gathers[2].third), (3, gathers[2].fourth),
                 (3, gathers[3].third),
             ):
-                pl.when(i == step)(event)
+                when(i == step, event)
 
             def slot(n):
                 j = 2 * i + n
                 at = pl.ds(slot_row(j), SLOT)
-                lanes = pl.ds(pl.multiple_of(j * SLOT, 128), SLOT)
+                lanes = lanes_of(j)
 
                 def put(value):
                     c_ref[at, :] = value
 
                 return block(n, xs_ref[at, :], slots.tag(j), 8 * seq + j, lanes, put)
 
-            together(slot(0), slot(1))
+            together(slot(0), slot(1), *more)
             return carry
 
-        lax.fori_loop(0, 4, two, 0)
-        together(
-            block(
-                0, slots.tail(xs_ref), slots.tail_tag(), slots.last_pair, pl.ds(8 * SLOT, TAIL),
-                functools.partial(slots.set_tail, c_ref),
-            )
+        lax.fori_loop(0, 3, two, 0)
+        tail = block(
+            2, slots.tail(xs_ref), slots.tail_tag(), slots.last_pair, pl.ds(8 * SLOT, TAIL),
+            functools.partial(slots.set_tail, c_ref),
         )
+        two(3, 0, tail)
 
     pl.run_scoped(
         forward,
         pltpu.VMEM((3 * D, D), bf16),
-        pltpu.VMEM((2, HEADS, SLOT, SLOT), f32),
-        pltpu.VMEM((2, HEADS, SLOT, SLOT), bf16),
-        pltpu.VMEM((2, SLOT, D), bf16),
-        pltpu.VMEM((2, D, SLOT), bf16),
+        pltpu.VMEM((3, HEADS, SLOT, SLOT), f32),
+        pltpu.VMEM((3, HEADS, SLOT, SLOT), bf16),
+        pltpu.VMEM((3, SLOT, D), bf16),
+        pltpu.VMEM((3, D, SLOT), bf16),
     )
     for i in (1, 2):
         gathers[i].finish()

time: 183 us -> 183 us (level)
  no operation moved by 1% of the time
where the time goes in v1:
time: 183 us
  Pallas kernels  182 us (99%)
    pallas_call x1, Pallas kernels, whole(): pl.pallas_call(whole_kernel, out_shape=out_shape, in_specs=[hbm] * 17 + [...  174 us
    pallas_call x1, Pallas kernels, last(): pl.pallas_call(last_kernel, out_shape=[shape(a.shape, a.dtype) for a in e...  8.32 us

profile of v1, /device:TPU:0, one launch (start us, length us, event | category | flops | bytes accessed | tf_op | source)
XLA Modules:
  0.0 183.0 jit_solution(8648890934009397125)
XLA Ops:
  0.7 173.8 %whole.1 = (bf16[2048,512]{1,0:T(8,128)(2,1)}, f32[2048,512]{1,0:T(8,128)}, f32[3,16,1536]{2,1,0:T(8,128)}, f32[3,16,512]{2,1,0:T(8,128)}, f32[3,16,2048]{2,1,0:...) custom-call(f32[16,1536]{1,0:T(8,128)} %refs_0_.1, ...), custom_call_target="tpu_custom_call" | custom-call | tf_op jit(solution)/shard_map/whole/pallas_call | solution.py:1575
  174.5 8.3 %last.1 = (bf16[2048,512]{1,0:T(8,128)(2,1)}, f32[2048,512]{1,0:T(8,128)}, f32[16,1536]{1,0:T(8,128)}, f32[16,512]{1,0:T(8,128)}, f32[16,2048]{1,0:T(8,128)}, /*...) custom-call(bf16[2048,512]{1,0:T(8,128)(2,1)} %get-tuple-element.58., ...), custom_call_target="tpu_custom_call" | custom-call | tf_op jit(solution)/shard_map/last/pallas_call | solution.py:1640
